TPU v7x, 32 devices: a whole 2x2x4 slice. The times are simulated.
32 devices in a mesh: parts: 2 (over x), rep: 2 (over core), tp: 8 (over z, y).
Axes of the slice: x: 2, y: 2, z: 4, core: 2. Of those that a mesh axis runs over, the one named last changes fastest.
Arguments:
- hidden: bfloat16 [4096, 28672], P(('parts', 'rep'), 'tp'), parts along dimension 0, may hold values from -6 to 6
- residual: bfloat16 [4096, 4096], P(('parts', 'rep', 'tp')), parts along dimension 0, may hold values from -6 to 6
- down_weight: bfloat16 [28672, 4096], P('tp'), may hold values from -0.03125 to 0.03125
- shrink_pool: bfloat16 [32, 64, 28672], P('rep', None, 'tp'), may hold values from -0.03125 to 0.03125
- expand_pool: bfloat16 [32, 64, 4096], P('rep', None, 'tp'), may hold values from -0.75 to 0.75
- seg_blocks: int32 [12], P('parts'), parts along dimension 0, may hold values from 1 to 8, 16 in all
- tail_rows: int32 [12], P('parts'), parts along dimension 0, may hold values from 1 to 128
- page_slot: int32 [12], P('parts'), parts along dimension 0, may hold values from 0 to 31, as said below
Outputs:
- mixed: bfloat16 [4096, 4096], P(('parts', 'rep', 'tp')), parts along dimension 0
There are 2 independent parts, one for each index of `parts`. A program takes and returns all parts, laid end to end along the dimension named above; an argument that names none is the same for every part. Nothing has to cross between parts.
Inputs may be any that keep to these rules, and one draw needn't show every extreme that they name: `page_slot`: the 6 pages are distinct; both page 0 and page 32 - 1 are among them.
All inputs are finite; a program needn't handle non-finite values.
Results may differ from a plain program's by a relative error of at most 0.01.
Values may be sent and summed in bfloat16 or wider, within the bound.
A program may use at most 192 MiB of HBM per device.

v0:
```python
import jax
import jax.numpy as jnp
from jax import lax
from jax.sharding import PartitionSpec as P

BLOCK = 128


ADAPTER_SCALE = 0.5


def block_table(seg_blocks, tail_rows, page_slot, block_count, block_len):
    seg_ends = jnp.cumsum(seg_blocks, dtype=jnp.int32)
    block_ids = jnp.arange(block_count, dtype=jnp.int32)
    segment = jnp.sum(
        (block_ids[:, None] >= seg_ends[None, :]).astype(jnp.int32), axis=1, dtype=jnp.int32
    )
    one_hot = (
        segment[:, None] == jnp.arange(seg_blocks.shape[0], dtype=jnp.int32)[None, :]
    ).astype(jnp.int32)
    page_lookup = jnp.sum(one_hot * page_slot[None, :], axis=1, dtype=jnp.int32)
    last_block = jnp.sum(one_hot * seg_ends[None, :], axis=1, dtype=jnp.int32) - 1
    tail_of = jnp.sum(one_hot * tail_rows[None, :], axis=1, dtype=jnp.int32)
    active_rows = jnp.where(block_ids == last_block, tail_of, block_len)
    return (page_lookup, active_rows, segment)


def body(hidden, residual, down_weight, shrink_pool, expand_pool, seg_blocks, tail_rows, page_slot):
    rep_count = lax.axis_size("rep")
    tp_count = lax.axis_size("tp")
    rep_index = lax.axis_index("rep")
    tp_index = lax.axis_index("tp")
    repeated_rows = hidden.shape[0]
    blk_rep = repeated_rows // BLOCK
    every_page, every_live, every_segment = block_table(
        seg_blocks, tail_rows, page_slot, rep_count * blk_rep, BLOCK
    )
    every_page = every_page.reshape(rep_count, blk_rep)
    every_live = every_live.reshape(rep_count, blk_rep)
    every_segment = every_segment.reshape(rep_count, blk_rep)
    page_lookup = lax.dynamic_index_in_dim(every_page, rep_index, 0, keepdims=False)
    active_rows = lax.dynamic_index_in_dim(every_live, rep_index, 0, keepdims=False)
    all_shrink, all_expand = (
        lax.all_gather(shrink_pool, "rep", axis=0, tiled=True),
        lax.all_gather(expand_pool, "rep", axis=0, tiled=True),
    )
    shrink_pages = jnp.take(all_shrink, page_lookup, axis=0)
    expand_pages = jnp.take(all_expand, page_lookup, axis=0)
    block_list = hidden.reshape(blk_rep, BLOCK, hidden.shape[1])
    shrink_part = jnp.einsum(
        "bnf,bkf->bnk", block_list, shrink_pages, preferred_element_type=jnp.float32
    )
    rank_rows = lax.psum(shrink_part.astype(jnp.bfloat16), "tp")
    expanded_rows = jnp.einsum(
        "bnk,bkc->bnc", rank_rows, expand_pages, preferred_element_type=jnp.float32
    )
    active_row_mask = (jnp.arange(BLOCK, dtype=jnp.int32)[None, :] < active_rows[:, None]).astype(
        jnp.float32
    )
    adapter_delta = (ADAPTER_SCALE * expanded_rows * active_row_mask[:, :, None]).reshape(
        repeated_rows, expanded_rows.shape[2]
    )
    out_rows = repeated_rows // tp_count
    full_partial = jnp.dot(hidden, down_weight, preferred_element_type=jnp.float32)
    every_sum = lax.psum(full_partial.astype(jnp.bfloat16), "tp").astype(jnp.float32)
    summed_output = lax.dynamic_slice_in_dim(every_sum, tp_index * out_rows, out_rows, 0)
    summed_output = summed_output + lax.all_to_all(
        adapter_delta.astype(jnp.bfloat16), "tp", split_axis=0, concat_axis=1, tiled=True
    ).astype(adapter_delta.dtype)
    return (residual.astype(jnp.float32) + summed_output).astype(jnp.bfloat16)


def solution(mesh):
    return jax.shard_map(
        body,
        mesh=mesh,
        in_specs=(
            P(("parts", "rep"), "tp"),
            P(("parts", "rep", "tp"), None),
            P("tp", None),
            P("rep", None, "tp"),
            P("rep", None, "tp"),
            P("parts"),
            P("parts"),
            P("parts"),
        ),
        out_specs=P(("parts", "rep", "tp"), None),
        check_vma=False,
    )
```

profile of v0, /device:TPU:0, one launch (start us, length us, event | category | flops | bytes accessed | tf_op | source)
XLA Modules:
  0.0 381.1 jit_solution(471283766563684359)
XLA Ops:
  6.5 0.0 all-gather.3.cloned.1.call-start
  6.5 0.7 all-gather.3.cloned.1.call-update
  7.3 0.0 all-gather.5.cloned.1.call-start
  7.3 0.7 all-gather.5.cloned.1.call-update
  8.0 0.0 copy-start.3
  8.0 0.0 copy-start.1
  8.0 0.0 copy-start.2
  8.0 0.0 all-reduce.3.cloned.1.call-start
  8.1 37.5 %convolution_convert_fusion = bf16[1024,4096]{1,0:T(8,128)(2,1)} fusion(bf16[1024,3584]{1,0:T(8,128)(2,1)} %param.8, bf16[3584,4096]{1,0:T(8,128)(2,1)} %param.10), kind=kOutput, calls=%fused_computation.2 | convolution fusion | flops 30068965376 | bytes 45088768 | tf_op jit(solution)/shard_map/dot_general | solution.py:64
  45.6 0.0 copy-done.3
  45.6 0.2 reduce-window.8
  45.8 0.1 convert_reduce_fusion
  45.9 0.0 copy-done.1
  45.9 0.0 copy-done.2
  45.9 0.1 select_reduce_fusion.1
  46.0 0.1 reshape.107
  46.1 0.0 all-gather.3.cloned.1.call-done
  46.1 8.9 %gather_fusion = bf16[8,64,3584]{2,1,0:T(8,128)(2,1)} fusion(bf16[32,64,3584]{2,1,0:T(8,128)(2,1)} %all-gather.3.cloned.1.call-done, s32[1024]{0:T(1024)S(1)} %pad_clamp_fusion), kind=kCustom, calls=%fused_computation | custom fusion | bytes 7340064 | tf_op jit(solution)/shard_map/jit(_take)/gather | solution.py:47
  55.0 7.5 %fusion.7 = bf16[8,128,64]{1,2,0:T(8,128)(2,1)} fusion(bf16[8,128,3584]{2,1,0:T(8,128)(2,1)} %bitcast.24, bf16[8,64,3584]{2,1,0:T(8,128)(2,1)} %gather_fusion, pred[8]{0:T(512)(128)(4,1)S(1)} %compare_and_fusion), kind=kOutput, calls=%fused_computation.11 | convolution fusion | flops 471662592 | bytes 11141128 | tf_op jit(solution)/shard_map/bnf,bkf->bnk/dot_general | solution.py:50
  62.6 0.0 all-reduce.3.cloned.1.call-update
  62.6 0.1 sub.6
  62.7 0.1 reduce_sum.42
  62.8 0.1 fusion.13
  62.8 2.2 gather_fusion.1
  65.0 274.6 %all-reduce.3.cloned.1.call-done = (bf16[8,128,64]{1,2,0:T(8,128)(2,1)}, bf16[1024,4096]{1,0:T(8,128)(2,1)}) async-done(((bf16[8,128,64]{1,2,0:T(8,128)(2,1)}, bf16[1024,4096]{1,0:T(8,128)(2,1)}), (bf16[8,128,64]{1,2,0:T(8,128)(2,1)}, bf16[1024,4096]{1,0:T(8,128)(2,1)})) %all-reduce.3.cloned.1.call-update) | async-done | bytes 8519696 | tf_op jit(solution)/shard_map/psum | solution.py:53
  339.6 2.4 multiply_convert_fusion
  342.0 3.6 all-to-all-start
  345.6 25.9 %all-to-all-done = bf16[8,128,512]{2,1,0:T(8,128)(2,1)S(1)} async-done(((bf16[8,128,512]{2,1,0:T(8,128)(2,1)}), bf16[8,128,512]{2,1,0:T(8,128)(2,1)S(1)}, u32[]{:S(2)}, u32[]{:S(2)}) %all-to-all-start) | async-done | bytes 1048608 | tf_op jit(solution)/shard_map/all_to_all | solution.py:67
  371.5 0.3 convert_bitcast_fusion
  371.8 0.2 copy.12
  372.0 0.0 copy-done
  372.0 2.6 add_convert_fusion
  (8 shorter events, 0.1 us)
Async XLA Ops:
  6.5 39.6 %all-gather.3.cloned.1.call-start = ((), (), s32[]{:S(2)}) async-start(), calls=%async_computation.1 | async-start | bytes 22020096 | tf_op jit(solution)/shard_map/all_gather | solution.py:44
  7.3 55.6 %all-gather.5.cloned.1.call-start = ((), (), s32[]{:S(2)}) async-start(), calls=%async_computation.2 | async-start | bytes 3145728 | tf_op jit(solution)/shard_map/all_gather | solution.py:45
  8.0 37.6 %copy-start.3 = (s32[6]{0:T(128)S(1)}, s32[6]{0:T(128)}, u32[]{:S(2)}) copy-start(s32[6]{0:T(128)} %param.13) | copy-start | bytes 76
  8.0 37.9 %copy-start.1 = (s32[6]{0:T(128)S(1)}, s32[6]{0:T(128)}, u32[]{:S(2)}) copy-start(s32[6]{0:T(128)} %param.14) | copy-start | bytes 76
  8.0 37.9 %copy-start.2 = (s32[6]{0:T(128)S(1)}, s32[6]{0:T(128)}, u32[]{:S(2)}) copy-start(s32[6]{0:T(128)} %param.15) | copy-start | bytes 76
  8.0 331.6 %all-reduce.3.cloned.1.call-start = ((), (), s32[]{:S(2)}) async-start(), calls=%async_computation.3 | async-start | bytes 17039360 | tf_op jit(solution)/shard_map/psum | solution.py:53
  342.0 29.5 %all-to-all-start = ((bf16[8,128,512]{2,1,0:T(8,128)(2,1)}), bf16[8,128,512]{2,1,0:T(8,128)(2,1)S(1)}, u32[]{:S(2)}, u32[]{:S(2)}) async-start(bf16[8,128,512]{2,1,0:T(8,128)(2,1)} %multiply_convert_fusion), calls=%async_computation | async-start | bytes 2097152 | tf_op jit(solution)/shard_map/all_to_all | solution.py:67
  345.6 26.4 %copy-start = (bf16[128,4096]{1,0:T(8,128)(2,1)S(1)}, bf16[128,4096]{1,0:T(8,128)(2,1)}, u32[]{:S(2)}) copy-start(bf16[128,4096]{1,0:T(8,128)(2,1)} %param.9) | copy-start | bytes 3145732
Sparse Core Ops, SparseCore 0:
  8.9 29.7 all-gather.2
  40.2 11.7 all-gather.4
  62.7 276.8 all-reduce.2
where the time goes:
time: 381 us
  waiting for transfers between devices  302 us (79%)
  matrix products  47.4 us (12%)
  between operations  13.2 us (3%)
  local copies, waits for them, and re-layouts  11.5 us (3%)
    psum x1, waiting for transfers between devices, body(): rank_rows = lax.psum(shrink_part.astype(jnp.bfloat16), 'tp')  275 us
    dot_general x1, matrix products, body(): jnp.dot(hidden, down_weight, preferred_element_type=jnp.float32)  37.5 us
    all_to_all x1, waiting for transfers between devices, body(): lax.all_to_all(adapter_delta.astype(jnp.bfloat16), 'tp', split_axis=0, co...  25.9 us
    gather x1, local copies, waits for them, and re-layouts, body(): shrink_pages = jnp.take(all_shrink, page_lookup, axis=0)  8.88 us
  transfers between devices with their start and end apart: 4, of which 2 were waited for; matrix products, arithmetic and copies ran while one was open for 15% of the time, Pallas kernels for 0%

commit v1 on v0

v1 whole, which is shorter than its diff:
```python
import functools

import jax
import jax.numpy as jnp
from jax import lax
from jax.experimental import pallas as pl
from jax.experimental.pallas import tpu as pltpu
from jax.sharding import PartitionSpec as P

BLOCK = 128
ADAPTER_SCALE = 0.5
MESH = pl.DeviceIdType.MESH
F32 = jnp.float32
BF16 = jnp.bfloat16


def block_table(seg_blocks, tail_rows, page_slot, block_count, block_len):
    seg_ends = jnp.cumsum(seg_blocks, dtype=jnp.int32)
    block_ids = jnp.arange(block_count, dtype=jnp.int32)
    segment = jnp.sum(
        (block_ids[:, None] >= seg_ends[None, :]).astype(jnp.int32), axis=1, dtype=jnp.int32
    )
    one_hot = (
        segment[:, None] == jnp.arange(seg_blocks.shape[0], dtype=jnp.int32)[None, :]
    ).astype(jnp.int32)
    page_lookup = jnp.sum(one_hot * page_slot[None, :], axis=1, dtype=jnp.int32)
    last_block = jnp.sum(one_hot * seg_ends[None, :], axis=1, dtype=jnp.int32) - 1
    tail_of = jnp.sum(one_hot * tail_rows[None, :], axis=1, dtype=jnp.int32)
    active_rows = jnp.where(block_ids == last_block, tail_of, block_len)
    return (page_lookup, active_rows, one_hot)


def pick_kernel(index_ref, owned_ref, shrink_ref, expand_ref, s_ref, e_ref):
    owned = owned_ref[pl.program_id(0)] > 0
    s_ref[...] = jnp.where(owned, shrink_ref[...], jnp.zeros_like(shrink_ref))
    e_ref[...] = jnp.where(owned, expand_ref[...], jnp.zeros_like(expand_ref))


def pick_pages(index, owned, shrink_pool, expand_pool):
    segs = index.shape[0]
    _, rank, depth = shrink_pool.shape
    width = expand_pool.shape[2]
    return pl.pallas_call(
        pick_kernel,
        grid_spec=pltpu.PrefetchScalarGridSpec(
            num_scalar_prefetch=2,
            grid=(segs,),
            in_specs=[
                pl.BlockSpec((1, rank, depth), lambda i, idx, own: (idx[i], 0, 0)),
                pl.BlockSpec((1, rank, width), lambda i, idx, own: (idx[i], 0, 0)),
            ],
            out_specs=[
                pl.BlockSpec((1, rank, depth), lambda i, idx, own: (i, 0, 0)),
                pl.BlockSpec((1, rank, width), lambda i, idx, own: (i, 0, 0)),
            ],
        ),
        out_shape=[
            jax.ShapeDtypeStruct((segs, rank, depth), BF16),
            jax.ShapeDtypeStruct((segs, rank, width), BF16),
        ],
    )(index, owned, shrink_pool, expand_pool)


def main_kernel(
    tp, nz, tiles, rank,
    hid, weight, residual, s_own, e_own, oh, live, out,
    hv, wbuf, ysend, yrecv, keep, rr, ll, acc, s_mine, s_recv, e_recv, page, page_in,
    rk, rk_in, res_buf,
    hv_sem, w_sem, misc_sem, rep_send, rep_recv,
    y_send, y_recv, r_send, r_recv, l_send, l_recv,
    pg_send, pg_recv, rk_send, rk_recv,
):
    t = lax.axis_index("tp")
    rep = lax.axis_index("rep")
    z = t // 2
    y = t % 2
    across = z * 2 + (1 - y)
    c = wbuf.shape[2]
    depth = wbuf.shape[1]
    segs_rank = s_mine.shape[0]
    chunk = e_own.shape[1]
    per_chunk = chunk // c

    def w_copy(i):
        slot = lax.rem(i, 3)
        cols = pl.ds(pl.multiple_of(i * c, c), c)
        return pltpu.make_async_copy(weight.at[:, cols], wbuf.at[slot], w_sem.at[slot])

    def hv_copy(g):
        side = (1 - y) if g == 0 else y
        return pltpu.make_async_copy(hid.at[:, side], hv.at[g], hv_sem.at[g])

    hv_copy(0).start()
    w_copy(0).start()
    hv_copy(1).start()
    w_copy(1).start()
    s_copy = pltpu.make_async_copy(s_own, s_mine, misc_sem.at[0])
    res_copy = pltpu.make_async_copy(residual, res_buf, misc_sem.at[1])

    barrier = pltpu.get_barrier_semaphore()
    for j in range(1, tp):
        pl.semaphore_signal(
            barrier, inc=1, device_id={"tp": lax.rem(t + j, tp)}, device_id_type=MESH
        )
    pl.semaphore_signal(barrier, inc=1, device_id={"rep": 1 - rep}, device_id_type=MESH)
    pl.semaphore_wait(barrier, tp)

    e_swap = pltpu.make_async_remote_copy(
        src_ref=e_own, dst_ref=e_recv, send_sem=rep_send.at[0], recv_sem=rep_recv.at[0],
        device_id={"rep": 1 - rep}, device_id_type=MESH,
    )
    s_swap = pltpu.make_async_remote_copy(
        src_ref=s_own, dst_ref=s_recv, send_sem=rep_send.at[1], recv_sem=rep_recv.at[1],
        device_id={"rep": 1 - rep}, device_id_type=MESH,
    )
    e_swap.start()

    def y_copy(i):
        return pltpu.make_async_remote_copy(
            src_ref=ysend.at[i], dst_ref=yrecv.at[i],
            send_sem=y_send.at[i], recv_sem=y_recv.at[i],
            device_id={"tp": across}, device_id_type=MESH,
        )

    def right_copy(i, first, src):
        part = pl.ds(first, nz - first)
        return pltpu.make_async_remote_copy(
            src_ref=src.at[i, part], dst_ref=rr.at[i, part],
            send_sem=r_send.at[i], recv_sem=r_recv.at[i],
            device_id={"tp": lax.rem(t + 2, tp)}, device_id_type=MESH,
        )

    def left_copy(i, count, src):
        part = pl.ds(0, count)
        return pltpu.make_async_remote_copy(
            src_ref=src.at[i, part], dst_ref=ll.at[i, part],
            send_sem=l_send.at[i], recv_sem=l_recv.at[i],
            device_id={"tp": lax.rem(t + tp - 2, tp)}, device_id_type=MESH,
        )

    def product(g, w):
        value = jnp.dot(
            hv[g].reshape(nz * BLOCK, depth), w, preferred_element_type=F32
        )
        return value.astype(BF16).reshape(nz, BLOCK, c)

    def multiply(i):
        w_copy(i).wait()

        @pl.when(i + 2 < tiles)
        def _():
            w_copy(i + 2).start()

        slot = lax.rem(i, 3)
        ysend[i] = product(0, wbuf[slot])
        y_copy(i).start()

        @pl.when(i == 0)
        def _():
            hv_copy(1).wait()

        keep[i] = product(1, wbuf[slot])

    def add(i, d, other):
        return (keep[i, d].astype(F32) + other[i, d].astype(F32)).astype(BF16)

    def group(g):
        @pl.when(g < tiles)
        def _():
            y_copy(g).wait_recv()
            for d in range(nz):
                keep[g, d] = add(g, d, yrecv)

        for k in range(nz):
            i = g - k

            @pl.when((z == k) & (i >= 0) & (i < tiles))
            def _():
                if k > 0:
                    right_copy(i, k, keep).wait_recv()
                    for d in range(k + 1, nz):
                        rr[i, d] = add(i, d, rr)
                if k < nz - 1:
                    right_copy(i, k + 1, keep if k == 0 else rr).start()

            @pl.when((z == nz - 1 - k) & (i >= 0) & (i < tiles))
            def _():
                me = nz - 1 - k
                if k > 0:
                    left_copy(i, me + 1, keep).wait_recv()
                    for d in range(me):
                        ll[i, d] = add(i, d, ll)
                if me > 0:
                    left_copy(i, me, keep if k == 0 else ll).start()

        i = g - (nz - 1)

        @pl.when((i >= 0) & (i < tiles))
        def _():
            for k in range(nz):

                @pl.when(z == k)
                def _():
                    total = keep[i, k].astype(F32)
                    if k > 0:
                        total = total + rr[i, k].astype(F32)
                    if k < nz - 1:
                        total = total + ll[i, k].astype(F32)
                    acc[i] = total

    def page_copy(j):
        return pltpu.make_async_remote_copy(
            src_ref=page.at[lax.rem(t + j, tp)], dst_ref=page_in.at[j],
            send_sem=pg_send.at[j], recv_sem=pg_recv.at[j],
            device_id={"tp": lax.rem(t + j, tp)}, device_id_type=MESH,
        )

    def rank_copy(j):
        return pltpu.make_async_remote_copy(
            src_ref=rk.at[lax.rem(t + j, tp)], dst_ref=rk_in.at[j],
            send_sem=rk_send.at[j], recv_sem=rk_recv.at[j],
            device_id={"tp": lax.rem(t + j, tp)}, device_id_type=MESH,
        )

    def send_pages():
        e_swap.wait()
        row = lax.broadcasted_iota(jnp.int32, (rank, segs_rank), 0)
        col = lax.broadcasted_iota(jnp.int32, (rank, segs_rank), 1)
        diagonal = (lax.rem(col, rank) == row).astype(F32)
        both = e_own[...] + e_recv[...]

        @pl.loop(0, tp)
        def _(u):
            pick = (diagonal * oh[pl.ds(u, 1), :]).astype(BF16)
            page[u] = jnp.dot(pick, both, preferred_element_type=F32).astype(BF16)

        for j in range(1, tp):
            page_copy(j).start()

    def send_ranks():
        s_copy.wait()
        s_swap.wait()
        s_mine[...] = s_mine[...] + s_recv[...]
        row = lax.broadcasted_iota(jnp.int32, (segs_rank, BLOCK), 0)
        col = lax.broadcasted_iota(jnp.int32, (segs_rank, BLOCK), 1)
        fold = (lax.rem(row, rank) == col).astype(BF16)
        for g in range(2):
            side = (1 - y) if g == 0 else y
            sums = lax.dot_general(
                hv[g].reshape(nz * BLOCK, depth), s_mine[...], (((1,), (1,)), ((), ())),
                preferred_element_type=F32,
            )
            for d in range(nz):
                u = 2 * d + side
                chosen = (sums[d * BLOCK : (d + 1) * BLOCK] * oh[pl.ds(u, 1), :]).astype(BF16)
                rk[u] = jnp.dot(chosen, fold, preferred_element_type=F32).astype(BF16)
        for j in range(1, tp):
            rank_copy(j).start()

    def add_delta():
        total = rk[t].astype(F32)
        for j in range(1, tp):
            rank_copy(j).wait()
            total = total + rk_in[j].astype(F32)
        rows = (total.astype(BF16).astype(F32) * live[...]).astype(BF16)[:, :rank]
        res_copy.wait()
        for j in range(tp):
            if j > 0:
                page_copy(j).wait()
                factor = page_in[j]
            else:
                factor = page[t]
            delta = jnp.dot(rows, factor, preferred_element_type=F32)
            owner = lax.rem(t + tp - j, tp)
            for h in range(per_chunk):
                tile = owner * per_chunk + h
                cols = pl.ds(pl.multiple_of(tile * c, c), c)
                acc[tile] = acc[tile] + delta[:, h * c : (h + 1) * c]

    hv_copy(0).wait()
    half = tiles // 2

    @pl.loop(0, half)
    def _(i):
        multiply(2 * i)
        multiply(2 * i + 1)

        @pl.when(i == 0)
        def _():
            send_pages()
            s_swap.start()
            s_copy.start()
            res_copy.start()

        @pl.when(i > 0)
        def _():
            group(i - 1)

    send_ranks()

    @pl.loop(half - 1, tiles + nz - 1)
    def _(g):
        group(g)

    add_delta()
    for i in range(tiles):
        cols = slice(i * c, (i + 1) * c)
        out[:, cols] = (res_buf[:, cols].astype(F32) + acc[i]).astype(BF16)

    @pl.loop(0, tiles)
    def _(i):
        y_copy(i).wait_send()
        for k in range(nz):

            @pl.when(z == k)
            def _():
                if k < nz - 1:
                    right_copy(i, k + 1, rr).wait_send()
                if k > 0:
                    left_copy(i, k, ll).wait_send()


def fused(tp, rank, hidden, weight, residual, s_own, e_own, oh, live):
    rows, depth = hidden.shape
    width = weight.shape[1]
    nz = tp // 2
    c = min(256, e_own.shape[1])
    tiles = width // c
    segs_rank, chunk = e_own.shape
    hid = hidden.reshape(nz, 2, BLOCK, depth)
    hbm = pl.BlockSpec(memory_space=pl.ANY)
    vmem = pl.BlockSpec(memory_space=pltpu.VMEM)
    slab = pltpu.VMEM((tiles, nz, BLOCK, c), BF16)
    dma = pltpu.SemaphoreType.DMA
    return pl.pallas_call(
        functools.partial(main_kernel, tp, nz, tiles, rank),
        out_shape=jax.ShapeDtypeStruct((BLOCK, width), BF16),
        in_specs=[hbm, hbm, hbm, hbm, vmem, vmem, vmem],
        out_specs=vmem,
        scratch_shapes=[
            pltpu.VMEM((2, nz, BLOCK, depth), BF16),
            pltpu.VMEM((3, depth, c), BF16),
            slab, slab, slab, slab, slab,
            pltpu.VMEM((tiles, BLOCK, c), F32),
            pltpu.VMEM((segs_rank, depth), BF16),
            pltpu.VMEM((segs_rank, depth), BF16),
            pltpu.VMEM((segs_rank, chunk), BF16),
            pltpu.VMEM((tp, rank, chunk), BF16),
            pltpu.VMEM((tp, rank, chunk), BF16),
            pltpu.VMEM((tp, BLOCK, BLOCK), BF16),
            pltpu.VMEM((tp, BLOCK, BLOCK), BF16),
            pltpu.VMEM((BLOCK, width), BF16),
            dma((2,)), dma((3,)), dma((2,)), dma((2,)), dma((2,)),
            dma((tiles,)), dma((tiles,)), dma((tiles,)), dma((tiles,)), dma((tiles,)),
            dma((tiles,)),
            dma((tp,)), dma((tp,)), dma((tp,)), dma((tp,)),
        ],
        compiler_params=pltpu.CompilerParams(
            collective_id=0, has_side_effects=True, vmem_limit_bytes=60 * 1024 * 1024
        ),
        cost_estimate=pl.CostEstimate(
            flops=2 * rows * depth * (width + segs_rank),
            bytes_accessed=2 * depth * (width + rows),
            transcendentals=0,
        ),
    )(hid, weight, residual, s_own, e_own, oh, live)


def body_fused(hidden, residual, down_weight, shrink_pool, expand_pool, seg_blocks, tail_rows, page_slot):
    rep_count = lax.axis_size("rep")
    tp_count = lax.axis_size("tp")
    rep_index = lax.axis_index("rep")
    tp_index = lax.axis_index("tp")
    blk_rep = hidden.shape[0] // BLOCK
    pages_here, rank, depth = shrink_pool.shape
    segs = seg_blocks.shape[0]
    local = page_slot - rep_index * pages_here
    owned = ((local >= 0) & (local < pages_here)).astype(jnp.int32)
    local = jnp.clip(local, 0, pages_here - 1)
    s_own, e_own = pick_pages(local, owned, shrink_pool, expand_pool)
    _, every_live, one_hot = block_table(
        seg_blocks, tail_rows, page_slot, rep_count * blk_rep, BLOCK
    )
    one_hot = lax.dynamic_slice_in_dim(one_hot, rep_index * blk_rep, blk_rep, 0)
    oh = jnp.repeat(one_hot.astype(F32), rank, axis=1)
    live_rows = lax.dynamic_index_in_dim(
        every_live, rep_index * blk_rep + tp_index, 0, keepdims=False
    )
    row_ids = lax.broadcasted_iota(jnp.int32, (BLOCK, BLOCK), 0)
    live = jnp.where(row_ids < live_rows, ADAPTER_SCALE, 0.0).astype(F32)
    return fused(
        tp_count, rank, hidden, down_weight, residual,
        s_own.reshape(segs * rank, depth), e_own.reshape(segs * rank, -1), oh, live,
    )


def body_plain(hidden, residual, down_weight, shrink_pool, expand_pool, seg_blocks, tail_rows, page_slot):
    rep_count = lax.axis_size("rep")
    rep_index = lax.axis_index("rep")
    repeated_rows = hidden.shape[0]
    blk_rep = repeated_rows // BLOCK
    every_page, every_live, _ = block_table(
        seg_blocks, tail_rows, page_slot, rep_count * blk_rep, BLOCK
    )
    page_lookup = lax.dynamic_slice_in_dim(every_page, rep_index * blk_rep, blk_rep, 0)
    active_rows = lax.dynamic_slice_in_dim(every_live, rep_index * blk_rep, blk_rep, 0)
    all_shrink = lax.all_gather(shrink_pool, "rep", axis=0, tiled=True)
    all_expand = lax.all_gather(expand_pool, "rep", axis=0, tiled=True)
    shrink_pages = jnp.take(all_shrink, page_lookup, axis=0)
    expand_pages = jnp.take(all_expand, page_lookup, axis=0)
    block_list = hidden.reshape(blk_rep, BLOCK, hidden.shape[1])
    shrink_part = jnp.einsum("bnf,bkf->bnk", block_list, shrink_pages, preferred_element_type=F32)
    rank_rows = lax.psum(shrink_part.astype(BF16), "tp")
    expanded = jnp.einsum("bnk,bkc->bnc", rank_rows, expand_pages, preferred_element_type=F32)
    mask = (jnp.arange(BLOCK, dtype=jnp.int32)[None, :] < active_rows[:, None]).astype(F32)
    delta = (ADAPTER_SCALE * expanded * mask[:, :, None]).reshape(repeated_rows, -1)
    partial = jnp.dot(hidden, down_weight, preferred_element_type=F32).astype(BF16)
    total = lax.psum_scatter(partial, "tp", scatter_dimension=0, tiled=True).astype(F32)
    total = total + lax.all_to_all(
        delta.astype(BF16), "tp", split_axis=0, concat_axis=1, tiled=True
    ).astype(F32)
    return (residual.astype(F32) + total).astype(BF16)


def body(hidden, residual, *rest):
    tp_count = lax.axis_size("tp")
    pairs = lax.axis_size("rep") == 2 and tp_count in (4, 6, 8)
    if pairs and residual.shape[0] == BLOCK and hidden.shape[0] == tp_count * BLOCK:
        return body_fused(hidden, residual, *rest)
    return body_plain(hidden, residual, *rest)


def solution(mesh):
    return jax.shard_map(
        body,
        mesh=mesh,
        in_specs=(
            P(("parts", "rep"), "tp"),
            P(("parts", "rep", "tp"), None),
            P("tp", None),
            P("rep", None, "tp"),
            P("rep", None, "tp"),
            P("parts"),
            P("parts"),
            P("parts"),
        ),
        out_specs=P(("parts", "rep", "tp"), None),
        check_vma=False,
    )
```

time: 381 us -> 150 us (0.39)
  waiting for transfers between devices: 302 us -> 0 us
  Pallas kernels: 0 us -> 141 us
  matrix products: 47.4 us -> 0 us
  between operations: 13.2 us -> 0.02 us
  local copies, waits for them, and re-layouts: 11.5 us -> 4.34 us
    psum x1 -> x0, waiting for transfers between devices: 275 us -> none  [body(): rank_rows = lax.psum(shrink_part.astype(jnp.bfloat16), 'tp')]
    pallas_call x0 -> x2, Pallas kernels: none -> 141 us  [the longest x1 136 us: fused(): pl.pallas_call(functools.partial(main_kernel, tp, nz, tiles, rank), out_s...]
    dot_general x3 -> x0, matrix products: 47.4 us -> none  [the longest x1 37.5 us: body(): jnp.dot(hidden, down_weight, preferred_element_type=jnp.float32)]
    all_to_all x1 -> x0, waiting for transfers between devices: 25.9 us -> none  [body(): lax.all_to_all(adapter_delta.astype(jnp.bfloat16), 'tp', split_axis=0, co...]
    gather x2 -> x0, local copies, waits for them, and re-layouts: 11 us -> none  [the longest x1 8.88 us: body(): shrink_pages = jnp.take(all_shrink, page_lookup, axis=0)]
  transfers between devices with their start and end apart: 4 -> 0, of which waited for: 2 -> 0; matrix products, arithmetic and copies ran while one was open for 15% -> 0% of each run, Pallas kernels for 0% -> 0%
where the time goes in v1:
time: 150 us
  Pallas kernels  141 us (94%)
  other arithmetic  4.92 us (3%)
  local copies, waits for them, and re-layouts  4.34 us (3%)
    pallas_call x1, Pallas kernels, fused(): pl.pallas_call(functools.partial(main_kernel, tp, nz, tiles, rank), out_s...  136 us
    pallas_call x1, Pallas kernels, pick_pages(): pl.pallas_call(pick_kernel, grid_spec=pltpu.PrefetchScalarGridSpec(num_sc...  5.09 us

profile of v1, /device:TPU:0, one launch (start us, length us, event | category | flops | bytes accessed | tf_op | source)
XLA Modules:
  0.0 150.5 jit_solution(845305561058740139)
XLA Ops:
  0.0 0.8 reduce-window.8
  0.8 0.1 convert_reduce_fusion
  0.9 1.2 and_convert_fusion.owned_ref
  2.1 1.2 subtract_clamp_fusion.index_ref
  3.4 0.8 select_reduce_fusion.1
  4.2 0.6 dynamic_slice.8
  4.8 0.6 compare_select_fusion
  5.4 0.1 iota_compare_fusion
  5.5 0.1 broadcast_in_dim.21
  5.6 0.7 reshape.43.oh
  6.3 0.7 iota.18.live
  7.0 5.1 %shard_map.82 = (bf16[6,64,3584]{2,1,0:T(8,128)(2,1)}, bf16[6,64,512]{2,1,0:T(8,128)(2,1)}) custom-call(s32[6]{0:T(128)} %subtract_clamp_fusion.index_ref, s32[6]{0:T(128)} %and_convert_fusion.owned_ref, bf16[16,64,3584]{2,1,0:T(8,128)(2,1)} %shrink_ref.1, bf16[16,64,512]{2,1,0:T(8,128)(2,1)} %expand_ref.1), custom_call_target="tpu_custom_call" | custom-call | tf_op jit(solution)/shard_map/pallas_call | solution.py:43
  12.1 136.1 %shard_map.83 = bf16[128,4096]{1,0:T(8,128)(2,1)} custom-call(bf16[4,2,128,3584]{3,2,1,0:T(8,128)(2,1)} %bitcast.8, bf16[3584,4096]{1,0:T(8,128)(2,1)} %weight.1, bf16[128,4096]{1,0:T(8,128)(2,1)} %residual.1, bf16[384,3584]{1,0:T(8,128)(2,1)} %bitcast.9, bf16[384,512]{1,0:T(8,128)(2,1)} %bitcast.10, f32[8,384]{1,0:T(8,128)} %reshape.43.oh, ...), custom_call_target="tpu_custom_call" | custom-call | flops 32883343360 | bytes 36700160 | tf_op jit(solution)/shard_map/pallas_call | solution.py:335
  148.2 2.3 %copy.10 = bf16[128,4096]{1,0:T(8,128)(2,1)} copy(bf16[128,4096]{1,0:T(8,128)(2,1)} %shard_map.83) | data formatting | bytes 2097152
  (2 shorter events, 0.0 us)

commit v2 on v1

--- a/solution.py
+++ b/solution.py
@@ -30,44 +30,75 @@
     return (page_lookup, active_rows, one_hot)
 
 
-def pick_kernel(index_ref, owned_ref, shrink_ref, expand_ref, s_ref, e_ref):
-    owned = owned_ref[pl.program_id(0)] > 0
-    s_ref[...] = jnp.where(owned, shrink_ref[...], jnp.zeros_like(shrink_ref))
-    e_ref[...] = jnp.where(owned, expand_ref[...], jnp.zeros_like(expand_ref))
-
-
-def pick_pages(index, owned, shrink_pool, expand_pool):
-    segs = index.shape[0]
+def pick_kernel(
+    tp, seg_ref, tail_ref, slot_ref, shrink, expand, s_out, e_out, oh_ref, own_ref, live_ref, s_sem, e_sem
+):
+    rep = lax.axis_index("rep")
+    mine = rep * tp + lax.axis_index("tp")
+    pages_here, rank, _ = shrink.shape
+    segs = s_out.shape[0]
+    copies = []
+    for s in range(segs):
+        local = slot_ref[s] - rep * pages_here
+        local = jnp.minimum(jnp.maximum(local, 0), pages_here - 1)
+        copies.append(pltpu.make_async_copy(shrink.at[local], s_out.at[s], s_sem.at[s]))
+        copies.append(pltpu.make_async_copy(expand.at[local], e_out.at[s], e_sem.at[s]))
+    for copy in copies:
+        copy.start()
+    block = lax.broadcasted_iota(jnp.int32, oh_ref.shape, 0) + rep * tp
+    group = lax.broadcasted_iota(jnp.int32, oh_ref.shape, 1) // rank
+    own_group = lax.broadcasted_iota(jnp.int32, own_ref.shape, 0) // rank
+    oh = jnp.zeros(oh_ref.shape, F32)
+    own = jnp.zeros(own_ref.shape, F32)
+    limit = jnp.int32(BLOCK)
+    begin = jnp.int32(0)
+    for s in range(segs):
+        end = begin + seg_ref[s]
+        oh = jnp.where((group == s) & (block >= begin) & (block < end), 1.0, oh)
+        local = slot_ref[s] - rep * pages_here
+        here = jnp.where((local >= 0) & (local < pages_here), 1.0, 0.0)
+        own = jnp.where(own_group == s, here, own)
+        limit = jnp.where(mine == end - 1, tail_ref[s], limit)
+        begin = end
+    oh_ref[...] = oh
+    own_ref[...] = own
+    row = lax.broadcasted_iota(jnp.int32, live_ref.shape, 0)
+    live_ref[...] = jnp.where(row < limit, ADAPTER_SCALE, 0.0)
+    for copy in copies:
+        copy.wait()
+
+
+def pick_pages(tp, seg_blocks, tail_rows, page_slot, shrink_pool, expand_pool):
+    segs = seg_blocks.shape[0]
     _, rank, depth = shrink_pool.shape
     width = expand_pool.shape[2]
+    smem = pl.BlockSpec(memory_space=pltpu.SMEM)
+    hbm = pl.BlockSpec(memory_space=pl.ANY)
+    vmem = pl.BlockSpec(memory_space=pltpu.VMEM)
     return pl.pallas_call(
-        pick_kernel,
-        grid_spec=pltpu.PrefetchScalarGridSpec(
-            num_scalar_prefetch=2,
-            grid=(segs,),
-            in_specs=[
-                pl.BlockSpec((1, rank, depth), lambda i, idx, own: (idx[i], 0, 0)),
-                pl.BlockSpec((1, rank, width), lambda i, idx, own: (idx[i], 0, 0)),
-            ],
-            out_specs=[
-                pl.BlockSpec((1, rank, depth), lambda i, idx, own: (i, 0, 0)),
-                pl.BlockSpec((1, rank, width), lambda i, idx, own: (i, 0, 0)),
-            ],
-        ),
+        functools.partial(pick_kernel, tp),
+        in_specs=[smem, smem, smem, hbm, hbm],
+        out_specs=[hbm, hbm, vmem, vmem, vmem],
         out_shape=[
             jax.ShapeDtypeStruct((segs, rank, depth), BF16),
             jax.ShapeDtypeStruct((segs, rank, width), BF16),
+            jax.ShapeDtypeStruct((tp, segs * rank), F32),
+            jax.ShapeDtypeStruct((segs * rank, 128), F32),
+            jax.ShapeDtypeStruct((BLOCK, rank), F32),
         ],
-    )(index, owned, shrink_pool, expand_pool)
+        scratch_shapes=[pltpu.SemaphoreType.DMA((segs,)), pltpu.SemaphoreType.DMA((segs,))],
+    )(seg_blocks, tail_rows, page_slot, shrink_pool, expand_pool)
 
 
 def main_kernel(
-    tp, nz, tiles, rank,
-    hid, weight, residual, s_own, e_own, oh, live, out,
-    hv, wbuf, ysend, yrecv, keep, rr, ll, acc, s_mine, s_recv, e_recv, page, page_in,
-    rk, rk_in, res_buf,
+    tp, nz, tiles, nb, rank,
+    hid, weight, residual, s_own, e_own, oh, own, live, out,
+    hv, wbuf, ysend, yrecv, keep, rr, ll, keep_b, rr_b, ll_b, ysend_b, yrecv_b,
+    acc, delta_buf, s_mine, s_recv, e_recv, page, page_in,
+    rk, rk_in, res_buf, e_mine,
     hv_sem, w_sem, misc_sem, rep_send, rep_recv,
     y_send, y_recv, r_send, r_recv, l_send, l_recv,
+    yb_send, yb_recv, rb_send, rb_recv, lb_send, lb_recv,
     pg_send, pg_recv, rk_send, rk_recv,
 ):
     t = lax.axis_index("tp")
@@ -80,6 +111,7 @@
     segs_rank = s_mine.shape[0]
     chunk = e_own.shape[1]
     per_chunk = chunk // c
+    na = tiles - nb
 
     def w_copy(i):
         slot = lax.rem(i, 3)
@@ -95,6 +127,8 @@
     hv_copy(1).start()
     w_copy(1).start()
     s_copy = pltpu.make_async_copy(s_own, s_mine, misc_sem.at[0])
+    e_copy = pltpu.make_async_copy(e_own, e_mine, misc_sem.at[2])
+    e_copy.start()
     res_copy = pltpu.make_async_copy(residual, res_buf, misc_sem.at[1])
 
     barrier = pltpu.get_barrier_semaphore()
@@ -138,34 +172,65 @@
             device_id={"tp": lax.rem(t + tp - 2, tp)}, device_id_type=MESH,
         )
 
+    def y_copy_b(b):
+        return pltpu.make_async_remote_copy(
+            src_ref=ysend_b.at[b], dst_ref=yrecv_b.at[b],
+            send_sem=yb_send.at[b], recv_sem=yb_recv.at[b],
+            device_id={"tp": across}, device_id_type=MESH,
+        )
+
+    def right_copy_b(b, first, src):
+        part = pl.ds(first, nz - first)
+        return pltpu.make_async_remote_copy(
+            src_ref=src.at[b, :, part], dst_ref=rr_b.at[b, :, part],
+            send_sem=rb_send.at[b], recv_sem=rb_recv.at[b],
+            device_id={"tp": lax.rem(t + 2, tp)}, device_id_type=MESH,
+        )
+
+    def left_copy_b(b, count, src):
+        part = pl.ds(0, count)
+        return pltpu.make_async_remote_copy(
+            src_ref=src.at[b, :, part], dst_ref=ll_b.at[b, :, part],
+            send_sem=lb_send.at[b], recv_sem=lb_recv.at[b],
+            device_id={"tp": lax.rem(t + tp - 2, tp)}, device_id_type=MESH,
+        )
+
     def product(g, w):
         value = jnp.dot(
             hv[g].reshape(nz * BLOCK, depth), w, preferred_element_type=F32
         )
         return value.astype(BF16).reshape(nz, BLOCK, c)
 
-    def multiply(i):
+    def next_weight(i):
         w_copy(i).wait()
 
         @pl.when(i + 2 < tiles)
         def _():
             w_copy(i + 2).start()
 
-        slot = lax.rem(i, 3)
-        ysend[i] = product(0, wbuf[slot])
-        y_copy(i).start()
+        return lax.rem(i, 3)
+
+    def multiply(i, a):
+        slot = next_weight(i)
+        ysend[a] = product(0, wbuf[slot])
+        y_copy(a).start()
 
         @pl.when(i == 0)
         def _():
             hv_copy(1).wait()
 
-        keep[i] = product(1, wbuf[slot])
+        keep[a] = product(1, wbuf[slot])
+
+    def multiply_b(i, b):
+        slot = next_weight(i)
+        for g in range(2):
+            keep_b[b, g] = product(g, wbuf[slot])
 
     def add(i, d, other):
         return (keep[i, d].astype(F32) + other[i, d].astype(F32)).astype(BF16)
 
     def group(g):
-        @pl.when(g < tiles)
+        @pl.when((g >= 0) & (g < na))
         def _():
             y_copy(g).wait_recv()
             for d in range(nz):
@@ -174,7 +239,7 @@
         for k in range(nz):
             i = g - k
 
-            @pl.when((z == k) & (i >= 0) & (i < tiles))
+            @pl.when((z == k) & (i >= 0) & (i < na))
             def _():
                 if k > 0:
                     right_copy(i, k, keep).wait_recv()
@@ -183,7 +248,7 @@
                 if k < nz - 1:
                     right_copy(i, k + 1, keep if k == 0 else rr).start()
 
-            @pl.when((z == nz - 1 - k) & (i >= 0) & (i < tiles))
+            @pl.when((z == nz - 1 - k) & (i >= 0) & (i < na))
             def _():
                 me = nz - 1 - k
                 if k > 0:
@@ -195,7 +260,7 @@
 
         i = g - (nz - 1)
 
-        @pl.when((i >= 0) & (i < tiles))
+        @pl.when((i >= 0) & (i < na))
         def _():
             for k in range(nz):
 
@@ -206,7 +271,63 @@
                         total = total + rr[i, k].astype(F32)
                     if k < nz - 1:
                         total = total + ll[i, k].astype(F32)
-                    acc[i] = total
+                    acc[jnp.where(i < nb, 2 * i, i + nb)] = total
+
+    def add_b(b, g, d, other):
+        return (keep_b[b, g, d].astype(F32) + other[b, g, d].astype(F32)).astype(BF16)
+
+    def group_b(i):
+        for k in range(nz):
+            b = i - 2 * k
+
+            @pl.when((z == k) & (b >= 0) & (b < nb))
+            def _():
+                if k > 0:
+                    right_copy_b(b, k, keep_b).wait_recv()
+                    for g in range(2):
+                        for d in range(k + 1, nz):
+                            rr_b[b, g, d] = add_b(b, g, d, rr_b)
+                if k < nz - 1:
+                    right_copy_b(b, k + 1, keep_b if k == 0 else rr_b).start()
+
+            @pl.when((z == nz - 1 - k) & (b >= 0) & (b < nb))
+            def _():
+                me = nz - 1 - k
+                if k > 0:
+                    left_copy_b(b, me + 1, keep_b).wait_recv()
+                    for g in range(2):
+                        for d in range(me):
+                            ll_b[b, g, d] = add_b(b, g, d, ll_b)
+                if me > 0:
+                    left_copy_b(b, me, keep_b if k == 0 else ll_b).start()
+
+        b = i - 2 * (nz - 1)
+
+        @pl.when((b >= 0) & (b < nb))
+        def _():
+            for k in range(nz):
+
+                @pl.when(z == k)
+                def _():
+                    for g in range(2):
+                        total = keep_b[b, g, k].astype(F32)
+                        if k > 0:
+                            total = total + rr_b[b, g, k].astype(F32)
+                        if k < nz - 1:
+                            total = total + ll_b[b, g, k].astype(F32)
+                        if g == 0:
+                            ysend_b[b] = total.astype(BF16)
+                        else:
+                            acc[2 * b + 1] = total
+
+            y_copy_b(b).start()
+
+        last = i - 2 * nz
+
+        @pl.when((last >= 0) & (last < nb))
+        def _():
+            y_copy_b(last).wait_recv()
+            acc[2 * last + 1] = acc[2 * last + 1] + yrecv_b[last].astype(F32)
 
     def page_copy(j):
         return pltpu.make_async_remote_copy(
@@ -223,11 +344,13 @@
         )
 
     def send_pages():
+        e_copy.wait()
         e_swap.wait()
         row = lax.broadcasted_iota(jnp.int32, (rank, segs_rank), 0)
         col = lax.broadcasted_iota(jnp.int32, (rank, segs_rank), 1)
         diagonal = (lax.rem(col, rank) == row).astype(F32)
-        both = e_own[...] + e_recv[...]
+        is_own = jnp.concatenate([own[...].astype(BF16)] * (chunk // 128), axis=1)
+        both = e_mine[...] * is_own + e_recv[...] * (1 - is_own)
 
         @pl.loop(0, tp)
         def _(u):
@@ -237,33 +360,51 @@
         for j in range(1, tp):
             page_copy(j).start()
 
-    def send_ranks():
+    def join_shrink():
         s_copy.wait()
         s_swap.wait()
-        s_mine[...] = s_mine[...] + s_recv[...]
-        row = lax.broadcasted_iota(jnp.int32, (segs_rank, BLOCK), 0)
-        col = lax.broadcasted_iota(jnp.int32, (segs_rank, BLOCK), 1)
-        fold = (lax.rem(row, rank) == col).astype(BF16)
-        for g in range(2):
-            side = (1 - y) if g == 0 else y
-            sums = lax.dot_general(
-                hv[g].reshape(nz * BLOCK, depth), s_mine[...], (((1,), (1,)), ((), ())),
-                preferred_element_type=F32,
-            )
-            for d in range(nz):
-                u = 2 * d + side
-                chosen = (sums[d * BLOCK : (d + 1) * BLOCK] * oh[pl.ds(u, 1), :]).astype(BF16)
-                rk[u] = jnp.dot(chosen, fold, preferred_element_type=F32).astype(BF16)
-        for j in range(1, tp):
-            rank_copy(j).start()
+        is_own = own[...].astype(BF16)
+
+        @pl.loop(0, depth // 128)
+        def _(i):
+            cols = pl.ds(pl.multiple_of(i * 128, 128), 128)
+            s_mine[:, cols] = s_mine[:, cols] * is_own + s_recv[:, cols] * (1 - is_own)
+
+    def rank_sums(g):
+        half_rows = BLOCK // 2
+        row = lax.rem(lax.broadcasted_iota(jnp.int32, (segs_rank, 2 * rank), 0), rank)
+        col = lax.broadcasted_iota(jnp.int32, (segs_rank, 2 * rank), 1)
+        top = (row == col).astype(BF16)
+        low = (row + rank == col).astype(BF16)
+        side = (1 - y) if g == 0 else y
+        sums = lax.dot_general(
+            hv[g].reshape(nz * BLOCK, depth), s_mine[...], (((1,), (1,)), ((), ())),
+            preferred_element_type=F32,
+        )
+        for d in range(nz):
+            u = 2 * d + side
+            chosen = (sums[d * BLOCK : (d + 1) * BLOCK] * oh[pl.ds(u, 1), :]).astype(BF16)
+            rk[u] = (
+                jnp.dot(chosen[:half_rows], top, preferred_element_type=F32)
+                + jnp.dot(chosen[half_rows:], low, preferred_element_type=F32)
+            ).astype(BF16)
 
     def add_delta():
         total = rk[t].astype(F32)
         for j in range(1, tp):
             rank_copy(j).wait()
             total = total + rk_in[j].astype(F32)
-        rows = (total.astype(BF16).astype(F32) * live[...]).astype(BF16)[:, :rank]
-        res_copy.wait()
+        total = total.astype(BF16)
+        row = lax.broadcasted_iota(jnp.int32, (2 * rank, rank), 0)
+        col = lax.broadcasted_iota(jnp.int32, (2 * rank, rank), 1)
+        rows = jnp.concatenate(
+            [
+                jnp.dot(total, (row == col).astype(BF16), preferred_element_type=F32),
+                jnp.dot(total, (row == col + rank).astype(BF16), preferred_element_type=F32),
+            ],
+            axis=0,
+        )
+        rows = (rows * live[...]).astype(BF16)
         for j in range(tp):
             if j > 0:
                 page_copy(j).wait()
@@ -273,41 +414,66 @@
             delta = jnp.dot(rows, factor, preferred_element_type=F32)
             owner = lax.rem(t + tp - j, tp)
             for h in range(per_chunk):
-                tile = owner * per_chunk + h
-                cols = pl.ds(pl.multiple_of(tile * c, c), c)
-                acc[tile] = acc[tile] + delta[:, h * c : (h + 1) * c]
-
+                delta_buf[owner * per_chunk + h] = delta[:, h * c : (h + 1) * c]
+        res_copy.wait()
+        for i in range(tiles):
+            delta_buf[i] = delta_buf[i] + res_buf[:, i * c : (i + 1) * c].astype(F32)
+
+    send_pages()
     hv_copy(0).wait()
     half = tiles // 2
 
     @pl.loop(0, half)
     def _(i):
-        multiply(2 * i)
-        multiply(2 * i + 1)
+        @pl.when(i < nb)
+        def _():
+            multiply(2 * i, i)
+            multiply_b(2 * i + 1, i)
+
+        @pl.when(i >= nb)
+        def _():
+            multiply(2 * i, 2 * i - nb)
+            multiply(2 * i + 1, 2 * i + 1 - nb)
 
         @pl.when(i == 0)
         def _():
-            send_pages()
             s_swap.start()
             s_copy.start()
             res_copy.start()
 
-        @pl.when(i > 0)
-        def _():
-            group(i - 1)
-
-    send_ranks()
-
-    @pl.loop(half - 1, tiles + nz - 1)
-    def _(g):
-        group(g)
+        group_b(i)
+        group(i - 1)
+
+        @pl.when(i == half - 3)
+        def _():
+            join_shrink()
+            rank_sums(0)
+
+        @pl.when(i == half - 2)
+        def _():
+            rank_sums(1)
+            for j in range(1, tp):
+                rank_copy(j).start()
+
+    steps = max(na + nz, nb + 2 * nz)
+    middle = (half + steps) // 2
+
+    @pl.loop(half, middle)
+    def _(i):
+        group_b(i)
+        group(i - 1)
 
     add_delta()
+
+    @pl.loop(middle, steps)
+    def _(i):
+        group_b(i)
+        group(i - 1)
+
     for i in range(tiles):
-        cols = slice(i * c, (i + 1) * c)
-        out[:, cols] = (res_buf[:, cols].astype(F32) + acc[i]).astype(BF16)
-
-    @pl.loop(0, tiles)
+        out[:, i * c : (i + 1) * c] = (delta_buf[i] + acc[i]).astype(BF16)
+
+    @pl.loop(0, na)
     def _(i):
         y_copy(i).wait_send()
         for k in range(nz):
@@ -319,8 +485,20 @@
                 if k > 0:
                     left_copy(i, k, ll).wait_send()
 
-
-def fused(tp, rank, hidden, weight, residual, s_own, e_own, oh, live):
+    @pl.loop(0, nb)
+    def _(b):
+        y_copy_b(b).wait_send()
+        for k in range(nz):
+
+            @pl.when(z == k)
+            def _():
+                if k < nz - 1:
+                    right_copy_b(b, k + 1, rr_b).wait_send()
+                if k > 0:
+                    left_copy_b(b, k, ll_b).wait_send()
+
+
+def fused(tp, rank, hidden, weight, residual, s_own, e_own, oh, own, live):
     rows, depth = hidden.shape
     width = weight.shape[1]
     nz = tp // 2
@@ -330,29 +508,36 @@
     hid = hidden.reshape(nz, 2, BLOCK, depth)
     hbm = pl.BlockSpec(memory_space=pl.ANY)
     vmem = pl.BlockSpec(memory_space=pltpu.VMEM)
-    slab = pltpu.VMEM((tiles, nz, BLOCK, c), BF16)
+    nb = (3 * tiles) // 16
+    na = tiles - nb
+    slab = pltpu.VMEM((na, nz, BLOCK, c), BF16)
+    slab_b = pltpu.VMEM((nb, 2, nz, BLOCK, c), BF16)
+    row_b = pltpu.VMEM((nb, BLOCK, c), BF16)
     dma = pltpu.SemaphoreType.DMA
     return pl.pallas_call(
-        functools.partial(main_kernel, tp, nz, tiles, rank),
+        functools.partial(main_kernel, tp, nz, tiles, nb, rank),
         out_shape=jax.ShapeDtypeStruct((BLOCK, width), BF16),
-        in_specs=[hbm, hbm, hbm, hbm, vmem, vmem, vmem],
+        in_specs=[hbm, hbm, hbm, hbm, hbm, vmem, vmem, vmem],
         out_specs=vmem,
         scratch_shapes=[
             pltpu.VMEM((2, nz, BLOCK, depth), BF16),
             pltpu.VMEM((3, depth, c), BF16),
             slab, slab, slab, slab, slab,
+            slab_b, slab_b, slab_b, row_b, row_b,
+            pltpu.VMEM((tiles, BLOCK, c), F32),
             pltpu.VMEM((tiles, BLOCK, c), F32),
             pltpu.VMEM((segs_rank, depth), BF16),
             pltpu.VMEM((segs_rank, depth), BF16),
             pltpu.VMEM((segs_rank, chunk), BF16),
             pltpu.VMEM((tp, rank, chunk), BF16),
             pltpu.VMEM((tp, rank, chunk), BF16),
-            pltpu.VMEM((tp, BLOCK, BLOCK), BF16),
-            pltpu.VMEM((tp, BLOCK, BLOCK), BF16),
+            pltpu.VMEM((tp, BLOCK // 2, 2 * rank), BF16),
+            pltpu.VMEM((tp, BLOCK // 2, 2 * rank), BF16),
             pltpu.VMEM((BLOCK, width), BF16),
-            dma((2,)), dma((3,)), dma((2,)), dma((2,)), dma((2,)),
-            dma((tiles,)), dma((tiles,)), dma((tiles,)), dma((tiles,)), dma((tiles,)),
-            dma((tiles,)),
+            pltpu.VMEM((segs_rank, chunk), BF16),
+            dma((2,)), dma((3,)), dma((3,)), dma((2,)), dma((2,)),
+            dma((na,)), dma((na,)), dma((na,)), dma((na,)), dma((na,)), dma((na,)),
+            dma((nb,)), dma((nb,)), dma((nb,)), dma((nb,)), dma((nb,)), dma((nb,)),
             dma((tp,)), dma((tp,)), dma((tp,)), dma((tp,)),
         ],
         compiler_params=pltpu.CompilerParams(
@@ -363,34 +548,19 @@
             bytes_accessed=2 * depth * (width + rows),
             transcendentals=0,
         ),
-    )(hid, weight, residual, s_own, e_own, oh, live)
+    )(hid, weight, residual, s_own, e_own, oh, own, live)
 
 
 def body_fused(hidden, residual, down_weight, shrink_pool, expand_pool, seg_blocks, tail_rows, page_slot):
-    rep_count = lax.axis_size("rep")
     tp_count = lax.axis_size("tp")
-    rep_index = lax.axis_index("rep")
-    tp_index = lax.axis_index("tp")
-    blk_rep = hidden.shape[0] // BLOCK
-    pages_here, rank, depth = shrink_pool.shape
     segs = seg_blocks.shape[0]
-    local = page_slot - rep_index * pages_here
-    owned = ((local >= 0) & (local < pages_here)).astype(jnp.int32)
-    local = jnp.clip(local, 0, pages_here - 1)
-    s_own, e_own = pick_pages(local, owned, shrink_pool, expand_pool)
-    _, every_live, one_hot = block_table(
-        seg_blocks, tail_rows, page_slot, rep_count * blk_rep, BLOCK
+    _, rank, depth = shrink_pool.shape
+    s_own, e_own, oh, own, live = pick_pages(
+        tp_count, seg_blocks, tail_rows, page_slot, shrink_pool, expand_pool
     )
-    one_hot = lax.dynamic_slice_in_dim(one_hot, rep_index * blk_rep, blk_rep, 0)
-    oh = jnp.repeat(one_hot.astype(F32), rank, axis=1)
-    live_rows = lax.dynamic_index_in_dim(
-        every_live, rep_index * blk_rep + tp_index, 0, keepdims=False
-    )
-    row_ids = lax.broadcasted_iota(jnp.int32, (BLOCK, BLOCK), 0)
-    live = jnp.where(row_ids < live_rows, ADAPTER_SCALE, 0.0).astype(F32)
     return fused(
         tp_count, rank, hidden, down_weight, residual,
-        s_own.reshape(segs * rank, depth), e_own.reshape(segs * rank, -1), oh, live,
+        s_own.reshape(segs * rank, depth), e_own.reshape(segs * rank, -1), oh, own, live,
     )
 
 
@@ -422,12 +592,13 @@
     return (residual.astype(F32) + total).astype(BF16)
 
 
-def body(hidden, residual, *rest):
+def body(hidden, residual, down_weight, shrink_pool, *rest):
     tp_count = lax.axis_size("tp")
     pairs = lax.axis_size("rep") == 2 and tp_count in (4, 6, 8)
+    pairs = pairs and 2 * shrink_pool.shape[1] == BLOCK
     if pairs and residual.shape[0] == BLOCK and hidden.shape[0] == tp_count * BLOCK:
-        return body_fused(hidden, residual, *rest)
-    return body_plain(hidden, residual, *rest)
+        return body_fused(hidden, residual, down_weight, shrink_pool, *rest)
+    return body_plain(hidden, residual, down_weight, shrink_pool, *rest)
 
 
 def solution(mesh):

time: 150 us -> 235 us (1.57)
  Pallas kernels: 141 us -> 233 us
  other arithmetic: 4.92 us -> 0 us
    pallas_call x2, Pallas kernels: 141 us -> 233 us  [the longest x1 135 us: fused(): pl.pallas_call(functools.partial(main_kernel, tp, nz, tiles, nb, rank), o...]
where the time goes in v2:
time: 235 us
  Pallas kernels  233 us (99%)
    pallas_call x1, Pallas kernels, fused(): pl.pallas_call(functools.partial(main_kernel, tp, nz, tiles, nb, rank), o...  135 us
    pallas_call x1, Pallas kernels, pick_pages(): pl.pallas_call(functools.partial(pick_kernel, tp), in_specs=[smem, smem,...  97.9 us

profile of v2, /device:TPU:0, one launch (start us, length us, event | category | flops | bytes accessed | tf_op | source)
XLA Modules:
  0.0 235.0 jit_solution(6262228958817668948)
XLA Ops:
  0.0 97.9 %shard_map.82 = (bf16[6,64,3584]{2,1,0:T(8,128)(2,1)}, bf16[6,64,512]{2,1,0:T(8,128)(2,1)}, f32[8,384]{1,0:T(8,128)}, f32[384,128]{1,0:T(8,128)}, f32[128,64]{1,0:T(8,128)}) custom-call(s32[6]{0:T(128)} %seg_ref.1, s32[6]{0:T(128)} %tail_ref.1, s32[6]{0:T(128)} %slot_ref.1, bf16[16,64,3584]{2,1,0:T(8,128)(2,1)} %shrink.1, bf16[16,64,512]{2,1,0:T(8,128)(2,1)} %expand.1), custom_call_target="tpu_custom_call" | custom-call | tf_op jit(solution)/shard_map/pallas_call | solution.py:78
  97.9 134.8 %shard_map.83 = bf16[128,4096]{1,0:T(8,128)(2,1)} custom-call(bf16[4,2,128,3584]{3,2,1,0:T(8,128)(2,1)} %bitcast.3, bf16[3584,4096]{1,0:T(8,128)(2,1)} %weight.1, bf16[128,4096]{1,0:T(8,128)(2,1)} %residual.1, bf16[384,3584]{1,0:T(8,128)(2,1)} %bitcast.4, bf16[384,512]{1,0:T(8,128)(2,1)} %bitcast.5, f32[8,384]{1,0:T(8,128)} %get-tuple-element.12.oh, ...), custom_call_target="tpu_custom_call" | custom-call | flops 32883343360 | bytes 36700160 | tf_op jit(solution)/shard_map/pallas_call | solution.py:517
  232.8 2.3 copy.10

commit v3 on v2

--- a/solution.py
+++ b/solution.py
@@ -31,7 +31,8 @@
 
 
 def pick_kernel(
-    tp, seg_ref, tail_ref, slot_ref, shrink, expand, s_out, e_out, oh_ref, own_ref, live_ref, s_sem, e_sem
+    tp, seg_ref, tail_ref, slot_ref, shrink, expand, s_out, e_out, oh_ref, own_ref, live_ref,
+    s_buf, e_buf, s_sem, e_sem, s_out_sem, e_out_sem
 ):
     rep = lax.axis_index("rep")
     mine = rep * tp + lax.axis_index("tp")
@@ -41,10 +42,20 @@
     for s in range(segs):
         local = slot_ref[s] - rep * pages_here
         local = jnp.minimum(jnp.maximum(local, 0), pages_here - 1)
-        copies.append(pltpu.make_async_copy(shrink.at[local], s_out.at[s], s_sem.at[s]))
-        copies.append(pltpu.make_async_copy(expand.at[local], e_out.at[s], e_sem.at[s]))
-    for copy in copies:
-        copy.start()
+        copies.append(
+            (
+                pltpu.make_async_copy(shrink.at[local], s_buf.at[s], s_sem.at[s]),
+                pltpu.make_async_copy(s_buf.at[s], s_out.at[s], s_out_sem.at[s]),
+            )
+        )
+        copies.append(
+            (
+                pltpu.make_async_copy(expand.at[local], e_buf.at[s], e_sem.at[s]),
+                pltpu.make_async_copy(e_buf.at[s], e_out.at[s], e_out_sem.at[s]),
+            )
+        )
+    for load, _ in copies:
+        load.start()
     block = lax.broadcasted_iota(jnp.int32, oh_ref.shape, 0) + rep * tp
     group = lax.broadcasted_iota(jnp.int32, oh_ref.shape, 1) // rank
     own_group = lax.broadcasted_iota(jnp.int32, own_ref.shape, 0) // rank
@@ -64,8 +75,11 @@
     own_ref[...] = own
     row = lax.broadcasted_iota(jnp.int32, live_ref.shape, 0)
     live_ref[...] = jnp.where(row < limit, ADAPTER_SCALE, 0.0)
-    for copy in copies:
-        copy.wait()
+    for load, store in copies:
+        load.wait()
+        store.start()
+    for _, store in copies:
+        store.wait()
 
 
 def pick_pages(tp, seg_blocks, tail_rows, page_slot, shrink_pool, expand_pool):
@@ -86,7 +100,11 @@
             jax.ShapeDtypeStruct((segs * rank, 128), F32),
             jax.ShapeDtypeStruct((BLOCK, rank), F32),
         ],
-        scratch_shapes=[pltpu.SemaphoreType.DMA((segs,)), pltpu.SemaphoreType.DMA((segs,))],
+        scratch_shapes=[
+            pltpu.VMEM((segs, rank, depth), BF16),
+            pltpu.VMEM((segs, rank, width), BF16),
+        ]
+        + [pltpu.SemaphoreType.DMA((segs,))] * 4,
     )(seg_blocks, tail_rows, page_slot, shrink_pool, expand_pool)
 
 
@@ -106,7 +124,8 @@
     z = t // 2
     y = t % 2
     across = z * 2 + (1 - y)
-    c = wbuf.shape[2]
+    c = wbuf.shape[2] // 2
+    half = tiles // 2
     depth = wbuf.shape[1]
     segs_rank = s_mine.shape[0]
     chunk = e_own.shape[1]
@@ -114,8 +133,8 @@
     na = tiles - nb
 
     def w_copy(i):
-        slot = lax.rem(i, 3)
-        cols = pl.ds(pl.multiple_of(i * c, c), c)
+        slot = lax.rem(i, 2)
+        cols = pl.ds(pl.multiple_of(i * 2 * c, 2 * c), 2 * c)
         return pltpu.make_async_copy(weight.at[:, cols], wbuf.at[slot], w_sem.at[slot])
 
     def hv_copy(g):
@@ -125,7 +144,6 @@
     hv_copy(0).start()
     w_copy(0).start()
     hv_copy(1).start()
-    w_copy(1).start()
     s_copy = pltpu.make_async_copy(s_own, s_mine, misc_sem.at[0])
     e_copy = pltpu.make_async_copy(e_own, e_mine, misc_sem.at[2])
     e_copy.start()
@@ -199,32 +217,38 @@
         value = jnp.dot(
             hv[g].reshape(nz * BLOCK, depth), w, preferred_element_type=F32
         )
-        return value.astype(BF16).reshape(nz, BLOCK, c)
-
-    def next_weight(i):
+        return value.astype(BF16).reshape(nz, BLOCK, 2 * c)
+
+    def multiply_pair(i, a, b):
+        slot = lax.rem(i, 2)
         w_copy(i).wait()
 
-        @pl.when(i + 2 < tiles)
-        def _():
-            w_copy(i + 2).start()
-
-        return lax.rem(i, 3)
-
-    def multiply(i, a):
-        slot = next_weight(i)
-        ysend[a] = product(0, wbuf[slot])
-        y_copy(a).start()
+        @pl.when(i + 1 < half)
+        def _():
+            w_copy(i + 1).start()
+
+        away = product(0, wbuf[slot])
+        ysend[a] = away[:, :, :c]
+        if b is None:
+            ysend[a + 1] = away[:, :, c:]
+
+            @pl.when(i == nb)
+            def _():
+                y_copy(a).start()
+        else:
+            y_copy(a).start()
+            keep_b[b, 0] = away[:, :, c:]
 
         @pl.when(i == 0)
         def _():
             hv_copy(1).wait()
 
-        keep[a] = product(1, wbuf[slot])
-
-    def multiply_b(i, b):
-        slot = next_weight(i)
-        for g in range(2):
-            keep_b[b, g] = product(g, wbuf[slot])
+        home = product(1, wbuf[slot])
+        keep[a] = home[:, :, :c]
+        if b is None:
+            keep[a + 1] = home[:, :, c:]
+        else:
+            keep_b[b, 1] = home[:, :, c:]
 
     def add(i, d, other):
         return (keep[i, d].astype(F32) + other[i, d].astype(F32)).astype(BF16)
@@ -233,6 +257,11 @@
         @pl.when((g >= 0) & (g < na))
         def _():
             y_copy(g).wait_recv()
+
+            @pl.when((g + 2 > nb) & (g + 2 < na))
+            def _():
+                y_copy(g + 2).start()
+
             for d in range(nz):
                 keep[g, d] = add(g, d, yrecv)
 
@@ -421,19 +450,16 @@
 
     send_pages()
     hv_copy(0).wait()
-    half = tiles // 2
 
     @pl.loop(0, half)
     def _(i):
         @pl.when(i < nb)
         def _():
-            multiply(2 * i, i)
-            multiply_b(2 * i + 1, i)
+            multiply_pair(i, i, i)
 
         @pl.when(i >= nb)
         def _():
-            multiply(2 * i, 2 * i - nb)
-            multiply(2 * i + 1, 2 * i + 1 - nb)
+            multiply_pair(i, 2 * i - nb, None)
 
         @pl.when(i == 0)
         def _():
@@ -521,7 +547,7 @@
         out_specs=vmem,
         scratch_shapes=[
             pltpu.VMEM((2, nz, BLOCK, depth), BF16),
-            pltpu.VMEM((3, depth, c), BF16),
+            pltpu.VMEM((2, depth, 2 * c), BF16),
             slab, slab, slab, slab, slab,
             slab_b, slab_b, slab_b, row_b, row_b,
             pltpu.VMEM((tiles, BLOCK, c), F32),
@@ -535,7 +561,7 @@
             pltpu.VMEM((tp, BLOCK // 2, 2 * rank), BF16),
             pltpu.VMEM((BLOCK, width), BF16),
             pltpu.VMEM((segs_rank, chunk), BF16),
-            dma((2,)), dma((3,)), dma((3,)), dma((2,)), dma((2,)),
+            dma((2,)), dma((2,)), dma((3,)), dma((2,)), dma((2,)),
             dma((na,)), dma((na,)), dma((na,)), dma((na,)), dma((na,)), dma((na,)),
             dma((nb,)), dma((nb,)), dma((nb,)), dma((nb,)), dma((nb,)), dma((nb,)),
             dma((tp,)), dma((tp,)), dma((tp,)), dma((tp,)),

time: 235 us -> 136 us (0.58)
  Pallas kernels: 233 us -> 133 us
    pallas_call x1, Pallas kernels: 97.9 us -> 5.16 us  [pick_pages(): pl.pallas_call(functools.partial(pick_kernel, tp), in_specs=[smem, smem,...]
    pallas_call x1, Pallas kernels: 135 us -> 128 us  [fused(): pl.pallas_call(functools.partial(main_kernel, tp, nz, tiles, nb, rank), o...]
where the time goes in v3:
time: 136 us
  Pallas kernels  133 us (98%)
  local copies, waits for them, and re-layouts  2.29 us (2%)
    pallas_call x1, Pallas kernels, fused(): pl.pallas_call(functools.partial(main_kernel, tp, nz, tiles, nb, rank), o...  128 us
    pallas_call x1, Pallas kernels, pick_pages(): pl.pallas_call(functools.partial(pick_kernel, tp), in_specs=[smem, smem,...  5.16 us

profile of v3, /device:TPU:0, one launch (start us, length us, event | category | flops | bytes accessed | tf_op | source)
XLA Modules:
  0.0 135.7 jit_solution(4620162816268913237)
XLA Ops:
  0.0 5.2 %shard_map.82 = (bf16[6,64,3584]{2,1,0:T(8,128)(2,1)}, bf16[6,64,512]{2,1,0:T(8,128)(2,1)}, f32[8,384]{1,0:T(8,128)}, f32[384,128]{1,0:T(8,128)}, f32[128,64]{1,0:T(8,128)}) custom-call(s32[6]{0:T(128)} %seg_ref.1, s32[6]{0:T(128)} %tail_ref.1, s32[6]{0:T(128)} %slot_ref.1, bf16[16,64,3584]{2,1,0:T(8,128)(2,1)} %shrink.1, bf16[16,64,512]{2,1,0:T(8,128)(2,1)} %expand.1), custom_call_target="tpu_custom_call" | custom-call | tf_op jit(solution)/shard_map/pallas_call | solution.py:92
  5.2 128.3 %shard_map.83 = bf16[128,4096]{1,0:T(8,128)(2,1)} custom-call(bf16[4,2,128,3584]{3,2,1,0:T(8,128)(2,1)} %bitcast.3, bf16[3584,4096]{1,0:T(8,128)(2,1)} %weight.1, bf16[128,4096]{1,0:T(8,128)(2,1)} %residual.1, bf16[384,3584]{1,0:T(8,128)(2,1)} %bitcast.4, bf16[384,512]{1,0:T(8,128)(2,1)} %bitcast.5, f32[8,384]{1,0:T(8,128)} %get-tuple-element.12.oh, ...), custom_call_target="tpu_custom_call" | custom-call | flops 32883343360 | bytes 36700160 | tf_op jit(solution)/shard_map/pallas_call | solution.py:543
  133.5 2.3 %copy.10 = bf16[128,4096]{1,0:T(8,128)(2,1)} copy(bf16[128,4096]{1,0:T(8,128)(2,1)} %shard_map.83) | data formatting | bytes 2097152
